TPU v7x, 32 devices: a whole 2x2x4 slice. The times are simulated.
32 devices in a mesh: seq: 16 (over z, x, core), head: 2 (over y).
Axes of the slice: x: 2, y: 2, z: 4, core: 2. Of those that a mesh axis runs over, the one named last changes fastest.
Arguments:
- rotated_queries: bfloat16 [8192, 4096], P(('seq', 'head')), may hold values from -6 to 6
- rotated_keys: bfloat16 [8192, 2048], P(('seq', 'head')), may hold values from -6 to 6
- value_matrix: bfloat16 [8192, 2048], P(('seq', 'head')), may hold values from -6 to 6
- output_rows: bfloat16 [8192, 4096], P(('seq', 'head')), may hold values from -6 to 6
- output_gradient: bfloat16 [8192, 4096], P(('seq', 'head')), may hold values from -6 to 6
- softmax_log_total: float32 [32, 8192], P(None, ('seq', 'head')), may hold values from 4 to 7
- doc_ids: int32 [8192], replicated, may hold values from 0 to 8, never falling along the last dimension, each value on 1 to 2048 neighbouring positions
Outputs:
- query_grad: bfloat16 [8192, 4096], P('seq', 'head')
- key_grad: bfloat16 [8192, 2048], P('seq', 'head')
- value_grad: bfloat16 [8192, 2048], P('seq', 'head')
Inputs may be any that keep to these rules, and one draw needn't show every extreme that they name: `doc_ids`: ids never fall from one token to the next; no document is longer than 2048 tokens.
All inputs are finite; a program needn't handle non-finite values.
Results may differ from a plain program's by a relative error of at most 0.0055.
Values may be sent and summed in bfloat16 or wider, within the bound.
A program may use at most 128 MiB of HBM per device.

v0:
```python
import jax
import jax.numpy as jnp
from jax import lax
from jax.sharding import PartitionSpec as P

HEAD_SIZE = 128
LOOKBACK_SPAN = 1024


score_scale = 168.0 ** (-0.5)


def shifted(value, axis, steps):
    count = lax.axis_size(axis)
    leading, last = (max(0, -steps), min(count, count - steps))
    return lax.ppermute(value, axis, [(source, source + steps) for source in range(leading, last)])


def tile_mask(doc_ids, query_start, key_start, row_count, number_of_tokens):
    query_pos = query_start + jnp.arange(row_count, dtype=jnp.int32)
    key_pos = key_start + jnp.arange(row_count, dtype=jnp.int32)
    query_doc = lax.dynamic_slice_in_dim(
        doc_ids, jnp.clip(query_start, 0, number_of_tokens - row_count), row_count, 0
    )
    key_doc = lax.dynamic_slice_in_dim(
        doc_ids, jnp.clip(key_start, 0, number_of_tokens - row_count), row_count, 0
    )
    gap = query_pos[:, None] - key_pos[None, :]
    inside = (
        (key_pos[None, :] >= 0)
        & (query_pos[:, None] < number_of_tokens)
        & (gap >= 0)
        & (gap < LOOKBACK_SPAN)
    )
    return inside & (query_doc[:, None] == key_doc[None, :])


def tile_terms(
    query_piece, gradient_piece, logsumexp_piece, delta_piece, key_piece, value_piece, allowed
):
    row_count = query_piece.shape[0]
    col_count = key_piece.shape[0]
    key_heads = key_piece.shape[1] // HEAD_SIZE
    query_group_width = logsumexp_piece.shape[0] // key_heads
    query_four = query_piece.reshape(row_count, key_heads, query_group_width, HEAD_SIZE)
    grad_four = gradient_piece.reshape(row_count, key_heads, query_group_width, HEAD_SIZE)
    key_three = key_piece.reshape(col_count, key_heads, HEAD_SIZE)
    value_three = value_piece.reshape(col_count, key_heads, HEAD_SIZE)
    lse_three = logsumexp_piece.reshape(key_heads, query_group_width, row_count)[..., None]
    delta_three = delta_piece.reshape(key_heads, query_group_width, row_count)[..., None]
    scores = (
        jnp.einsum("rgad,cgd->garc", query_four, key_three, preferred_element_type=jnp.float32)
        * score_scale
    )
    prob_full = jnp.where(allowed[None, None], jnp.exp(scores - lse_three), 0.0)
    probability_narrow = prob_full.astype(jnp.bfloat16)
    prob_grad = jnp.einsum(
        "rgad,cgd->garc", grad_four, value_three, preferred_element_type=jnp.float32
    )
    score_gradient = (score_scale * prob_full * (prob_grad - delta_three)).astype(jnp.bfloat16)
    query_part = jnp.einsum(
        "garc,cgd->rgad", score_gradient, key_three, preferred_element_type=jnp.float32
    ).reshape(row_count, -1)
    key_portion = jnp.einsum(
        "plmw,mplo->wpo", score_gradient, query_four, preferred_element_type=jnp.float32
    ).reshape(col_count, -1)
    value_portion = jnp.einsum(
        "plmw,mplo->wpo", probability_narrow, grad_four, preferred_element_type=jnp.float32
    ).reshape(col_count, -1)
    return (query_part, key_portion, value_portion)


def on_device(
    rotated_queries,
    rotated_keys,
    value_matrix,
    output_rows,
    output_gradient,
    softmax_log_total,
    doc_ids,
):
    heads_all = softmax_log_total.shape[0]
    local_tokens = rotated_queries.shape[0]
    delta_rows = jnp.einsum(
        "thd,thd->ht",
        output_gradient.astype(jnp.float32).reshape(local_tokens, heads_all, HEAD_SIZE),
        output_rows.astype(jnp.float32).reshape(local_tokens, heads_all, HEAD_SIZE),
    )
    queries, keys, values, grads = (
        lax.all_to_all(rotated_queries, "head", split_axis=1, concat_axis=0, tiled=True),
        lax.all_to_all(rotated_keys, "head", split_axis=1, concat_axis=0, tiled=True),
        lax.all_to_all(value_matrix, "head", split_axis=1, concat_axis=0, tiled=True),
        lax.all_to_all(output_gradient, "head", split_axis=1, concat_axis=0, tiled=True),
    )
    lse_block, delta_block = (
        lax.all_to_all(softmax_log_total, "head", split_axis=0, concat_axis=1, tiled=True),
        lax.all_to_all(delta_rows, "head", split_axis=0, concat_axis=1, tiled=True),
    )
    row_count = queries.shape[0]
    number_of_tokens = doc_ids.shape[0]
    shard_index = lax.axis_index("seq")
    own_start = shard_index * row_count
    reach_count = LOOKBACK_SPAN // row_count

    def terms(
        query_piece,
        gradient_piece,
        logsumexp_piece,
        delta_piece,
        key_piece,
        value_piece,
        query_start,
        key_start,
    ):
        allowed = tile_mask(doc_ids, query_start, key_start, row_count, number_of_tokens)
        return tile_terms(
            query_piece,
            gradient_piece,
            logsumexp_piece,
            delta_piece,
            key_piece,
            value_piece,
            allowed,
        )

    query_grad, key_grad, value_grad = terms(
        queries, grads, lse_block, delta_block, keys, values, own_start, own_start
    )
    far_parts = []
    for offset in range(1, reach_count + 1):
        near_keys, near_values = shifted((keys, values), "seq", offset)
        query_part, key_portion, value_portion = terms(
            queries,
            grads,
            lse_block,
            delta_block,
            near_keys,
            near_values,
            own_start,
            own_start - offset * row_count,
        )
        query_grad = query_grad + query_part
        far_parts.append((key_portion, value_portion))
    for offset in range(1, reach_count + 1):
        back_keys, back_values = shifted(
            (far_parts[offset - 1][0], far_parts[offset - 1][1]), "seq", -offset
        )
        key_grad = key_grad + back_keys
        value_grad = value_grad + back_values
    return (
        query_grad.astype(jnp.bfloat16),
        key_grad.astype(jnp.bfloat16),
        value_grad.astype(jnp.bfloat16),
    )


def solution(mesh):
    return jax.shard_map(
        on_device,
        mesh=mesh,
        in_specs=(
            P(("seq", "head"), None),
            P(("seq", "head"), None),
            P(("seq", "head"), None),
            P(("seq", "head"), None),
            P(("seq", "head"), None),
            P(None, ("seq", "head")),
            P(),
        ),
        out_specs=(P("seq", "head"), P("seq", "head"), P("seq", "head")),
        check_vma=False,
    )
```

profile of v0, /device:TPU:1, one launch (start us, length us, event | category | flops | bytes accessed | tf_op | source)
XLA Modules:
  0.0 343.7 jit_solution(4793886320131449002)
XLA Ops:
  22.6 9.7 %all-to-all-done = bf16[256,2,1024]{0,2,1:T(8,128)(2,1)S(1)} async-done(((bf16[256,2,1024]{0,2,1:T(8,128)(2,1)}), bf16[256,2,1024]{0,2,1:T(8,128)(2,1)S(1)}, u32[]{:S(2)}, u32[]{:S(2)}) %all-to-all-start) | async-done | bytes 1048608 | tf_op jit(solution)/shard_map/all_to_all | solution.py:91
  39.9 8.0 %all-to-all-done.3 = bf16[256,2,1024]{0,2,1:T(8,128)(2,1)} async-done(((bf16[256,2,1024]{0,2,1:T(8,128)(2,1)}), bf16[256,2,1024]{0,2,1:T(8,128)(2,1)}, u32[]{:S(2)}, u32[]{:S(2)}) %all-to-all-start.3) | async-done | bytes 1048608 | tf_op jit(solution)/shard_map/all_to_all | solution.py:92
  47.9 4.8 %all-to-all-start.1 = ((bf16[256,2,2048]{2,0,1:T(8,128)(2,1)}), bf16[256,2,2048]{2,0,1:T(8,128)(2,1)}, u32[]{:S(2)}, u32[]{:S(2)}) async-start(bf16[256,2,2048]{2,0,1:T(8,128)(2,1)} %bitcast.189), calls=%async_computation.1 | async-start | bytes 4194304 | tf_op jit(solution)/shard_map/all_to_all | solution.py:90
  54.2 20.0 %all-to-all-done.1 = bf16[256,2,2048]{2,0,1:T(8,128)(2,1)} async-done(((bf16[256,2,2048]{2,0,1:T(8,128)(2,1)}), bf16[256,2,2048]{2,0,1:T(8,128)(2,1)}, u32[]{:S(2)}, u32[]{:S(2)}) %all-to-all-start.1) | async-done | bytes 2097184 | tf_op jit(solution)/shard_map/all_to_all | solution.py:90
  74.2 4.8 %all-to-all-start.4 = ((bf16[256,2,2048]{2,0,1:T(8,128)(2,1)}), bf16[256,2,2048]{2,0,1:T(8,128)(2,1)}, u32[]{:S(2)}, u32[]{:S(2)}) async-start(bf16[256,2,2048]{2,0,1:T(8,128)(2,1)} %bitcast.188), calls=%async_computation.4 | async-start | bytes 4194304 | tf_op jit(solution)/shard_map/all_to_all | solution.py:93
  88.5 7.0 %collective-permute-start.1 = (bf16[512,1024]{1,0:T(8,128)(2,1)}, bf16[512,1024]{1,0:T(8,128)(2,1)}, u32[]{:S(2)}, u32[]{:S(2)}) collective-permute-start(bf16[512,1024]{1,0:T(8,128)(2,1)} %bitcast.21), channel_id=1, source_target_pairs={{0,2},{2,4},{4,6},{6,8},{8,10},{10,12},{12,14},{14,16},{16,18},{18... | collective-permute-start | bytes 3145736 | tf_op jit(solution)/shard_map/ppermute | solution.py:16
  112.5 4.7 %copy.109 = bf16[512,8,2,128]{0,3,2,1:T(8,128)(2,1)S(1)} copy(bf16[512,8,2,128]{3,2,1,0:T(2,128)(2,1)} %reshape.377) | data formatting | bytes 4194304 | tf_op jit(solution)/shard_map/reshape | solution.py:45
  121.7 6.1 %copy.118 = bf16[512,8,2,128]{0,3,2,1:T(8,128)(2,1)} copy(bf16[512,8,2,128]{3,2,1,0:T(2,128)(2,1)} %reshape.379) | data formatting | bytes 4194304 | tf_op jit(solution)/shard_map/reshape | solution.py:46
  127.8 8.1 %fusion.44 = f32[8,512,512,2]{2,1,3,0:T(8,128)} fusion(bf16[512,8,128,1]{0,2,3,1:T(8,128)(2,1)S(1)} %copy.137, bf16[512,8,2,128]{0,3,2,1:T(8,128)(2,1)S(1)} %copy.109), kind=kOutput, calls=%fused_computation.64 | convolution fusion | flops 1073741824 | bytes 19922944 | tf_op jit(solution)/shard_map/rgad,cgd->garc/dot_general | solution.py:52
  136.0 11.4 %fusion.9 = bf16[8,2,512,512]{2,3,1,0:T(8,128)(2,1)} fusion(f32[8,512,512,2]{2,1,3,0:T(8,128)} %fusion.44, bf16[512,8,2,128]{0,3,2,1:T(8,128)(2,1)S(1)} %copy-done.8, f32[8,2,512]{2,1,0:T(2,128)S(1)} %sub.103, f32[8,2,512]{2,1,0:T(2,128)S(1)} %sub.100, pred[512,512]{0,1:T(8,128)(4,1)S(1)} %copy-done.11, bf16[512,8,128,1]{2,1,0,3:T(8,128)(2,1)S(1)} %bitcast.204), kind=kOutput, calls=%fused_computation.14 | convolution fusion | flops 1103101952 | bytes 28639232 | tf_op jit(solution)/shard_map/rgad,cgd->garc/dot_general | solution.py:57
  147.4 11.2 %fusion.19 = f32[8,512,128,1]{1,2,3,0:T(8,128)} fusion(bf16[512,8,2,128]{0,3,2,1:T(8,128)(2,1)} %copy.118, f32[8,512,512,2]{2,1,3,0:T(8,128)} %fusion.44, f32[8,2,512]{2,1,0:T(2,128)S(1)} %sub.100, pred[512,512]{0,1:T(8,128)(4,1)S(1)} %copy-done.12), kind=kOutput, calls=%fused_computation.23 | convolution fusion | flops 1090519040 | bytes 21266432 | tf_op jit(solution)/shard_map/plmw,mplo->wpo/dot_general | solution.py:67
  158.6 7.5 %fusion.47 = f32[8,512,128,1]{1,2,3,0:T(8,128)} fusion(bf16[8,2,512,512]{2,3,1,0:T(8,128)(2,1)} %fusion.9, bf16[512,8,2,128]{0,3,2,1:T(8,128)(2,1)S(1)} %copy.109), kind=kOutput, calls=%fused_computation.67 | convolution fusion | flops 1073741824 | bytes 12582912 | tf_op jit(solution)/shard_map/plmw,mplo->wpo/dot_general | solution.py:64
  167.8 8.1 %fusion.46 = f32[8,512,512,2]{2,1,3,0:T(8,128)} fusion(bf16[512,8,128,1]{0,2,3,1:T(8,128)(2,1)S(1)} %bitcast.181, bf16[512,8,2,128]{0,3,2,1:T(8,128)(2,1)S(1)} %copy.109), kind=kOutput, calls=%fused_computation.66 | convolution fusion | flops 1073741824 | bytes 19922944 | tf_op jit(solution)/shard_map/rgad,cgd->garc/dot_general | solution.py:52
  178.2 10.2 %fusion.1 = bf16[8,2,512,512]{2,3,1,0:T(8,128)(2,1)S(1)} fusion(f32[8,512,512,2]{2,1,3,0:T(8,128)} %fusion.46, bf16[512,8,128,1]{0,2,3,1:T(8,128)(2,1)} %bitcast.206, bf16[512,8,2,128]{0,3,2,1:T(8,128)(2,1)} %copy.118, f32[8,2,512]{2,1,0:T(2,128)S(1)} %sub.103, f32[8,2,512]{2,1,0:T(2,128)S(1)} %sub.100, pred[512,512]{0,1:T(8,128)(4,1)} %get-tuple-element.15), kind=kOutput, calls=%fused_computation.2 | convolution fusion | flops 1103101952 | bytes 28639232 | tf_op jit(solution)/shard_map/rgad,cgd->garc/dot_general | solution.py:57
  202.7 9.3 %fusion.45 = f32[8,512,512,2]{2,1,3,0:T(8,128)} fusion(bf16[512,8,128,1]{0,2,3,1:T(8,128)(2,1)} %bitcast.183, bf16[512,8,2,128]{0,3,2,1:T(8,128)(2,1)S(1)} %copy.109), kind=kOutput, calls=%fused_computation.65 | convolution fusion | flops 1073741824 | bytes 19922944 | tf_op jit(solution)/shard_map/rgad,cgd->garc/dot_general | solution.py:52
  212.0 11.3 %fusion.15 = f32[8,512,128,1]{1,2,3,0:T(8,128)} fusion(bf16[512,8,2,128]{0,3,2,1:T(8,128)(2,1)} %copy.118, f32[8,512,512,2]{2,1,3,0:T(8,128)} %fusion.46, f32[8,2,512]{2,1,0:T(2,128)S(1)} %sub.100, pred[512,512]{0,1:T(8,128)(4,1)} %get-tuple-element.15), kind=kOutput, calls=%fused_computation.21 | convolution fusion | flops 1090519040 | bytes 21266432 | tf_op jit(solution)/shard_map/plmw,mplo->wpo/dot_general | solution.py:67
  225.6 10.1 %fusion.5 = bf16[8,2,512,512]{2,3,1,0:T(8,128)(2,1)S(1)} fusion(f32[8,512,512,2]{2,1,3,0:T(8,128)} %fusion.45, bf16[512,8,128,1]{0,2,3,1:T(8,128)(2,1)} %bitcast.205, bf16[512,8,2,128]{0,3,2,1:T(8,128)(2,1)} %copy.118, f32[8,2,512]{2,1,0:T(2,128)S(1)} %sub.103, f32[8,2,512]{2,1,0:T(2,128)S(1)} %sub.100, pred[512,512]{0,1:T(8,128)(4,1)S(1)} %get-tuple-element.16), kind=kOutput, calls=%fused_computation.8 | convolution fusion | flops 1103101952 | bytes 28639232 | tf_op jit(solution)/shard_map/rgad,cgd->garc/dot_general | solution.py:57
  246.3 11.2 %fusion.17 = f32[8,512,128,1]{1,2,3,0:T(8,128)} fusion(bf16[512,8,2,128]{0,3,2,1:T(8,128)(2,1)} %copy.118, f32[8,512,512,2]{2,1,3,0:T(8,128)} %fusion.45, f32[8,2,512]{2,1,0:T(2,128)S(1)} %sub.100, pred[512,512]{0,1:T(8,128)(4,1)S(1)} %get-tuple-element.16), kind=kOutput, calls=%fused_computation.22 | convolution fusion | flops 1090519040 | bytes 21266432 | tf_op jit(solution)/shard_map/plmw,mplo->wpo/dot_general | solution.py:67
  266.7 6.7 %fusion.50 = f32[8,2,512,128]{2,3,1,0:T(8,128)} fusion(bf16[512,8,128,1]{0,2,3,1:T(8,128)(2,1)S(1)} %copy-done.4, bf16[8,2,512,512]{2,3,1,0:T(8,128)(2,1)} %fusion.9), kind=kOutput, calls=%fused_computation.70 | convolution fusion | flops 1073741824 | bytes 13631488 | tf_op jit(solution)/shard_map/garc,cgd->rgad/dot_general | solution.py:61
  279.2 4.8 %fusion.51 = f32[8,2,512,128]{2,3,1,0:T(8,128)S(1)} fusion(bf16[512,8,128,1]{0,2,3,1:T(8,128)(2,1)S(1)} %bitcast.184, bf16[8,2,512,512]{2,3,1,0:T(8,128)(2,1)} %copy-done.1), kind=kOutput, calls=%fused_computation.71 | convolution fusion | flops 1073741824 | bytes 13631488 | tf_op jit(solution)/shard_map/garc,cgd->rgad/dot_general | solution.py:61
  284.0 5.0 %add_convert_fusion = bf16[8,2,512,128]{2,3,1,0:T(8,128)(2,1)S(1)} fusion(f32[8,2,512,128]{2,3,1,0:T(8,128)S(1)} %copy-done.2, f32[8,2,512,128]{2,3,1,0:T(8,128)S(1)} %fusion.51, bf16[512,8,128,1]{0,2,3,1:T(8,128)(2,1)S(1)} %bitcast.182, bf16[8,2,512,512]{2,3,1,0:T(8,128)(2,1)} %copy-done), kind=kOutput, calls=%fused_computation.29 | convolution fusion | flops 1076887552 | bytes 19922944 | tf_op jit(solution)/shard_map/garc,cgd->rgad/dot_general | solution.py:61
  291.4 4.5 %add_convert_fusion.2 = bf16[512,1024]{1,0:T(8,128)(2,1)} fusion(f32[512,1024]{1,0:T(8,128)} %collective-permute-done.5, f32[512,1024]{1,0:T(8,128)} %copy.113, f32[512,1024]{1,0:T(8,128)} %collective-permute-done.4), kind=kLoop, calls=%fused_computation.33 | loop fusion | flops 1572864 | bytes 7340032 | tf_op jit(solution)/shard_map/convert_element_type | solution.py:152
  295.9 15.3 %collective-permute-done.7 = f32[512,1024]{1,0:T(8,128)} collective-permute-done((f32[512,1024]{1,0:T(8,128)}, f32[512,1024]{1,0:T(8,128)}, u32[]{:S(2)}, u32[]{:S(2)}) %collective-permute-start.7) | collective-permute-done | bytes 2097184 | tf_op jit(solution)/shard_map/ppermute | solution.py:16
  311.3 28.5 %collective-permute-done.6 = f32[512,1024]{1,0:T(8,128)} collective-permute-done((f32[512,1024]{1,0:T(8,128)}, f32[512,1024]{1,0:T(8,128)}, u32[]{:S(2)}, u32[]{:S(2)}) %collective-permute-start.6) | collective-permute-done | bytes 2097184 | tf_op jit(solution)/shard_map/ppermute | solution.py:16
  (84 shorter events, 114.0 us)
Async XLA Ops:
  0.6 12.8 %copy-start.9 = (bf16[256,2048]{1,0:T(8,128)(2,1)S(1)}, bf16[256,2048]{1,0:T(8,128)(2,1)}, u32[]{:S(2)}) copy-start(bf16[256,2048]{1,0:T(8,128)(2,1)} %param.8) | copy-start | bytes 3145732
  0.6 9.5 %all-to-all-start.2 = ((f32[2,16,256]{2,1,0:T(8,128)}), f32[2,16,256]{2,1,0:T(8,128)S(1)}, u32[]{:S(2)}, u32[]{:S(2)}) async-start(f32[2,16,256]{2,1,0:T(8,128)} %bitcast.209), calls=%async_computation.2 | async-start | bytes 65536 | tf_op jit(solution)/shard_map/all_to_all | solution.py:96
  10.1 6.6 %all-to-all-start.5 = ((f32[2,16,256]{2,1,0:T(8,128)}), f32[2,16,256]{2,1,0:T(8,128)S(1)}, u32[]{:S(2)}, u32[]{:S(2)}) async-start(f32[2,16,256]{2,1,0:T(8,128)} %bitcast.14), calls=%async_computation.5 | async-start | bytes 65536 | tf_op jit(solution)/shard_map/all_to_all | solution.py:97
  13.4 39.3 %copy-start.7 = (bf16[256,4096]{1,0:T(8,128)(2,1)S(1)}, bf16[256,4096]{1,0:T(8,128)(2,1)}, u32[]{:S(2)}) copy-start(bf16[256,4096]{1,0:T(8,128)(2,1)} %param.11) | copy-start | bytes 6291460
  16.7 15.6 %all-to-all-start = ((bf16[256,2,1024]{0,2,1:T(8,128)(2,1)}), bf16[256,2,1024]{0,2,1:T(8,128)(2,1)S(1)}, u32[]{:S(2)}, u32[]{:S(2)}) async-start(bf16[256,2,1024]{0,2,1:T(8,128)(2,1)} %bitcast.196), calls=%async_computation | async-start | bytes 2097152 | tf_op jit(solution)/shard_map/all_to_all | solution.py:91
  32.3 15.6 %all-to-all-start.3 = ((bf16[256,2,1024]{0,2,1:T(8,128)(2,1)}), bf16[256,2,1024]{0,2,1:T(8,128)(2,1)}, u32[]{:S(2)}, u32[]{:S(2)}) async-start(bf16[256,2,1024]{0,2,1:T(8,128)(2,1)} %bitcast.197), calls=%async_computation.3 | async-start | bytes 2097152 | tf_op jit(solution)/shard_map/all_to_all | solution.py:92
  47.9 26.3 %all-to-all-start.1 = ((bf16[256,2,2048]{2,0,1:T(8,128)(2,1)}), bf16[256,2,2048]{2,0,1:T(8,128)(2,1)}, u32[]{:S(2)}, u32[]{:S(2)}) async-start(bf16[256,2,2048]{2,0,1:T(8,128)(2,1)} %bitcast.189), calls=%async_computation.1 | async-start | bytes 4194304 | tf_op jit(solution)/shard_map/all_to_all | solution.py:90
  74.2 43.0 %all-to-all-start.4 = ((bf16[256,2,2048]{2,0,1:T(8,128)(2,1)}), bf16[256,2,2048]{2,0,1:T(8,128)(2,1)}, u32[]{:S(2)}, u32[]{:S(2)}) async-start(bf16[256,2,2048]{2,0,1:T(8,128)(2,1)} %bitcast.188), calls=%async_computation.4 | async-start | bytes 4194304 | tf_op jit(solution)/shard_map/all_to_all | solution.py:93
  84.9 91.0 %collective-permute-start.3 = (bf16[512,1024]{1,0:T(8,128)(2,1)}, bf16[512,1024]{1,0:T(8,128)(2,1)}, u32[]{:S(2)}, u32[]{:S(2)}) collective-permute-start(bf16[512,1024]{1,0:T(8,128)(2,1)} %bitcast.21), channel_id=1, source_target_pairs={{0,4},{2,6},{4,8},{6,10},{8,12},{10,14},{12,16},{14,18},{16,20},{1... | collective-permute-start | bytes 3145736 | tf_op jit(solution)/shard_map/ppermute | solution.py:16
  88.5 134.8 %collective-permute-start.1 = (bf16[512,1024]{1,0:T(8,128)(2,1)}, bf16[512,1024]{1,0:T(8,128)(2,1)}, u32[]{:S(2)}, u32[]{:S(2)}) collective-permute-start(bf16[512,1024]{1,0:T(8,128)(2,1)} %bitcast.21), channel_id=1, source_target_pairs={{0,2},{2,4},{4,6},{6,8},{8,10},{10,12},{12,14},{14,16},{16,18},{18... | collective-permute-start | bytes 3145736 | tf_op jit(solution)/shard_map/ppermute | solution.py:16
  96.9 69.3 %collective-permute-start.2 = (bf16[512,1024]{1,0:T(8,128)(2,1)}, bf16[512,1024]{1,0:T(8,128)(2,1)}, u32[]{:S(2)}, u32[]{:S(2)}) collective-permute-start(bf16[512,1024]{1,0:T(8,128)(2,1)} %bitcast.17), channel_id=1, source_target_pairs={{0,4},{2,6},{4,8},{6,10},{8,12},{10,14},{12,16},{14,18},{16,20},{1... | collective-permute-start | bytes 3145736 | tf_op jit(solution)/shard_map/ppermute | solution.py:16
  100.9 99.0 %collective-permute-start = (bf16[512,1024]{1,0:T(8,128)(2,1)}, bf16[512,1024]{1,0:T(8,128)(2,1)}, u32[]{:S(2)}, u32[]{:S(2)}) collective-permute-start(bf16[512,1024]{1,0:T(8,128)(2,1)} %bitcast.17), channel_id=1, source_target_pairs={{0,2},{2,4},{4,6},{6,8},{8,10},{10,12},{12,14},{14,16},{16,18},{18... | collective-permute-start | bytes 3145736 | tf_op jit(solution)/shard_map/ppermute | solution.py:16
  105.2 22.6 %copy-start.3 = (bf16[512,8,128,1]{0,2,3,1:T(8,128)(2,1)}, bf16[512,8,128,1]{0,2,3,1:T(8,128)(2,1)S(1)}, u32[]{:S(2)}) copy-start(bf16[512,8,128,1]{0,2,3,1:T(8,128)(2,1)S(1)} %copy.137) | copy-start | bytes 3145732
  127.8 8.1 %copy-start.8 = (bf16[512,8,2,128]{0,3,2,1:T(8,128)(2,1)S(1)}, bf16[512,8,2,128]{0,3,2,1:T(8,128)(2,1)}, u32[]{:S(2)}) copy-start(bf16[512,8,2,128]{0,3,2,1:T(8,128)(2,1)} %copy.118) | copy-start | bytes 6291460
  127.8 8.1 %copy-start.10 = (bf16[64,8,8,128]{3,2,1,0:T(8,128)(2,1)S(1)}, bf16[64,8,8,128]{3,2,1,0:T(8,128)(2,1)}, u32[]{:S(2)}) copy-start(bf16[64,8,8,128]{3,2,1,0:T(8,128)(2,1)} %copy.176) | copy-start | bytes 3145732
  127.8 8.1 %copy-start.11 = (pred[512,512]{0,1:T(8,128)(4,1)S(1)}, pred[512,512]{0,1:T(8,128)(4,1)}, u32[]{:S(2)}) copy-start(pred[512,512]{0,1:T(8,128)(4,1)} %get-tuple-element.17) | copy-start | bytes 786436
  136.0 11.4 %copy-start.12 = (pred[512,512]{0,1:T(8,128)(4,1)S(1)}, pred[512,512]{0,1:T(8,128)(4,1)}, u32[]{:S(2)}) copy-start(pred[512,512]{0,1:T(8,128)(4,1)} %get-tuple-element.17) | copy-start | bytes 786436
  198.7 92.7 %collective-permute-start.5 = (f32[512,1024]{1,0:T(8,128)}, f32[512,1024]{1,0:T(8,128)}, u32[]{:S(2)}, u32[]{:S(2)}) collective-permute-start(f32[512,1024]{1,0:T(8,128)} %copy.116), channel_id=1, source_target_pairs={{4,0},{6,2},{8,4},{10,6},{12,8},{14,10},{16,12},{18,14},{20,16},{2... | collective-permute-start | bytes 6291464 | tf_op jit(solution)/shard_map/ppermute | solution.py:16
  242.7 48.7 %collective-permute-start.4 = (f32[512,1024]{1,0:T(8,128)}, f32[512,1024]{1,0:T(8,128)}, u32[]{:S(2)}, u32[]{:S(2)}) collective-permute-start(f32[512,1024]{1,0:T(8,128)} %copy.112), channel_id=1, source_target_pairs={{2,0},{4,2},{6,4},{8,6},{10,8},{12,10},{14,12},{16,14},{18,16},{20... | collective-permute-start | bytes 6291464 | tf_op jit(solution)/shard_map/ppermute | solution.py:16
  257.5 9.2 %copy-start.4 = (bf16[512,8,128,1]{0,2,3,1:T(8,128)(2,1)S(1)}, bf16[512,8,128,1]{0,2,3,1:T(8,128)(2,1)}, u32[]{:S(2)}) copy-start(bf16[512,8,128,1]{0,2,3,1:T(8,128)(2,1)} %copy-done.3) | copy-start | bytes 3145732
  260.5 50.8 %collective-permute-start.7 = (f32[512,1024]{1,0:T(8,128)}, f32[512,1024]{1,0:T(8,128)}, u32[]{:S(2)}, u32[]{:S(2)}) collective-permute-start(f32[512,1024]{1,0:T(8,128)} %copy.125), channel_id=1, source_target_pairs={{4,0},{6,2},{8,4},{10,6},{12,8},{14,10},{16,12},{18,14},{20,16},{2... | collective-permute-start | bytes 6291464 | tf_op jit(solution)/shard_map/ppermute | solution.py:16
  264.7 14.5 %copy-start.5 = (bf16[512,1024]{0,1:T(8,128)(2,1)S(1)}, bf16[512,1024]{0,1:T(8,128)(2,1)}, u32[]{:S(2)}) copy-start(bf16[512,1024]{0,1:T(8,128)(2,1)} %copy.93) | copy-start | bytes 3145732
  264.7 75.1 %collective-permute-start.6 = (f32[512,1024]{1,0:T(8,128)}, f32[512,1024]{1,0:T(8,128)}, u32[]{:S(2)}, u32[]{:S(2)}) collective-permute-start(f32[512,1024]{1,0:T(8,128)} %copy.121), channel_id=1, source_target_pairs={{2,0},{4,2},{6,4},{8,6},{10,8},{12,10},{14,12},{16,14},{18,16},{20... | collective-permute-start | bytes 6291464 | tf_op jit(solution)/shard_map/ppermute | solution.py:16
  291.4 48.4 %copy-start.6 = (f32[512,1024]{1,0:T(8,128)S(1)}, f32[512,1024]{1,0:T(8,128)}, u32[]{:S(2)}) copy-start(f32[512,1024]{1,0:T(8,128)} %copy.122) | copy-start | bytes 6291460
  (3 other events, 12.2 us)
where the time goes:
time: 350 us; the launch traced here: 344 us
  matrix products  123 us (35%)
  waiting for transfers between devices  83.5 us (24%)
  local copies, waits for them, and re-layouts  73.6 us (21%)
  starting transfers between devices  49.3 us (14%)
  other arithmetic  12.9 us (4%)
    ppermute x8, waiting for transfers between devices, shifted(): lax.ppermute(value, axis, [(source, source + steps) for source in range(l...  43.9 us
    dot_general x3, matrix products, tile_terms(): jnp.einsum('plmw,mplo->wpo', probability_narrow, grad_four, preferred_ele...  33.7 us
    dot_general x3, matrix products, tile_terms(): jnp.einsum('rgad,cgd->garc', grad_four, value_three, preferred_element_ty...  31.6 us
    dot_general x3, matrix products, tile_terms(): jnp.einsum('rgad,cgd->garc', query_four, key_three, preferred_element_typ...  25.6 us
    ppermute x8, starting transfers between devices, shifted(): lax.ppermute(value, axis, [(source, source + steps) for source in range(l...  24.9 us
    all_to_all x1, waiting for transfers between devices, on_device(): lax.all_to_all(rotated_queries, 'head', split_axis=1, concat_axis=0, tile...  20 us
    unnamed x33, local copies, waits for them, and re-layouts  17.7 us
    dot_general x3, matrix products, tile_terms(): jnp.einsum('garc,cgd->rgad', score_gradient, key_three, preferred_element...  16.5 us
  transfers between devices with their start and end apart: 14, of which 6 were waited for; matrix products, arithmetic and copies ran while one was open for 59% of the time, Pallas kernels for 0%

commit v1 on v0

v1 whole, which is shorter than its diff:
```python
import functools
import math

import jax
import jax.numpy as jnp
from jax import lax
from jax.experimental import pallas as pl
from jax.experimental.pallas import tpu as pltpu
from jax.sharding import PartitionSpec as P

HEAD_SIZE = 128
LOOKBACK_SPAN = 1024
TILE = 256
SCORE_SCALE = 168.0 ** (-0.5)
LOG2E = math.log2(math.e)
MASKED = -1e30
MESH = pl.DeviceIdType.MESH
Y_LEAD = 4
HALO_LEAD = 2


def dot(a, b, contract):
    return lax.dot_general(a, b, ((contract[:1], contract[1:]), ((), ())), preferred_element_type=jnp.float32)


def kernel(
    shards, parts, heads,
    q_hbm, k_hbm, v_hbm, do_hbm, stats_hbm, docs_ref,
    dq_ref, dk_ref, dv_ref,
    kv, qd, stats, bias, own, acc, dqt, part, ret_a, ret_b, ret_c,
    y_send, y_recv, loc, st_send, st_recv, st_loc,
    near_send, near_recv, fardir_send, fwd_send, far_recv,
    p0_send, p1_send, a_recv, b_recv, c_recv,
):
    s = lax.axis_index("seq")
    y = lax.axis_index("head")
    even = lax.rem(s, 2) == 0
    rows = k_hbm.shape[0]
    block = rows * parts
    near_rows = pl.ds(block, block)
    far_rows = pl.ds(0, block)
    own_rows = pl.ds(2 * block, block)

    def at(seq, head):
        return {"seq": seq, "head": head}

    barrier = pltpu.get_barrier_semaphore()
    for step in range(1, parts):
        pl.semaphore_signal(barrier, inc=1, device_id=at(s, lax.rem(y + step, parts)), device_id_type=MESH)
    has_prev, has_next = s >= 1, s < shards - 1
    even_prev = even & (s >= 2)
    even_next = even & (s + 2 < shards)
    for cond, other in ((has_prev, s - 1), (has_next, s + 1), (even_prev, s - 2), (even_next, s + 2)):

        @pl.when(cond)
        def _():
            pl.semaphore_signal(barrier, inc=1, device_id=at(other, y), device_id_type=MESH)

    peers = parts - 1
    for cond in (has_prev, has_next, even_prev, even_next):
        peers = peers + jnp.where(cond, 1, 0)
    pl.semaphore_wait(barrier, peers)

    half = (y * rows) // TILE
    inner = pl.multiple_of(lax.rem(y * rows, TILE), rows)
    token_row = pl.multiple_of(2 * block + y * rows, rows)

    def pieces(g, target):
        head = target * heads + g
        col = pl.ds(pl.multiple_of(head * HEAD_SIZE, HEAD_SIZE), HEAD_SIZE)
        found = [
            (k_hbm.at[:, col], kv.at[g, 0, pl.ds(token_row, rows), :]),
            (v_hbm.at[:, col], kv.at[g, 1, pl.ds(token_row, rows), :]),
        ]
        for source, slot in ((q_hbm, 0), (do_hbm, 1)):
            for j in range(2):
                qcol = pl.ds(pl.multiple_of((head * 2 + j) * HEAD_SIZE, HEAD_SIZE), HEAD_SIZE)
                found.append((source.at[:, qcol], qd.at[g, slot, half, j, pl.ds(inner, rows), :]))
        return found

    def y_copies(g, which):
        found = []
        for step in range(1, parts):
            target = lax.rem(y + step, parts)
            for n, (src, dst) in enumerate(pieces(g, target)):
                if n in which:
                    found.append(
                        pltpu.make_async_remote_copy(
                            src_ref=src, dst_ref=dst,
                            send_sem=y_send.at[g, step, n], recv_sem=y_recv.at[g, step, n],
                            device_id=at(s, target), device_id_type=MESH,
                        )
                    )
        return found

    def local_copies(g, which):
        return [
            pltpu.make_async_copy(src, dst, loc.at[g, n])
            for n, (src, dst) in enumerate(pieces(g, y))
            if n in which
        ]

    KV_PIECES, Q_PIECES = (0, 1), (2, 3, 4, 5)

    def y_start(g, which):
        for copy in y_copies(g, which):
            copy.start()
        for copy in local_copies(g, which):
            copy.start()

    def y_arrive(g, which):
        for step in range(1, parts):
            source = lax.rem(y + parts - step, parts)
            their_half = (source * rows) // TILE
            their_inner = pl.multiple_of(lax.rem(source * rows, TILE), rows)
            their_row = pl.multiple_of(2 * block + source * rows, rows)
            for n, (src, _) in enumerate(pieces(g, y)):
                if n not in which:
                    continue
                if n < 2:
                    dst = kv.at[g, n, pl.ds(their_row, rows), :]
                else:
                    dst = qd.at[g, (n - 2) // 2, their_half, (n - 2) % 2, pl.ds(their_inner, rows), :]
                pltpu.make_async_remote_copy(
                    src_ref=src, dst_ref=dst,
                    send_sem=y_send.at[g, step, n], recv_sem=y_recv.at[g, step, n],
                    device_id=at(s, source), device_id_type=MESH,
                ).wait_recv()
        for copy in local_copies(g, which):
            copy.wait()

    def stat_copy(step, mine):
        other = lax.rem(y + step, parts)
        source = y if mine else lax.rem(y + parts - step, parts)
        return pltpu.make_async_remote_copy(
            src_ref=stats_hbm.at[other], dst_ref=stats.at[source],
            send_sem=st_send.at[step], recv_sem=st_recv.at[step],
            device_id=at(s, other), device_id_type=MESH,
        )

    def remote(src, dst, send, recv, target):
        return pltpu.make_async_remote_copy(
            src_ref=src, dst_ref=dst, send_sem=send, recv_sem=recv,
            device_id=at(target, y), device_id_type=MESH,
        )

    def near(g):
        return remote(kv.at[g, :, own_rows, :], kv.at[g, :, near_rows, :], near_send.at[g], near_recv.at[g], s + 1)

    def far_direct(g):
        return remote(kv.at[g, :, own_rows, :], kv.at[g, :, far_rows, :], fardir_send.at[g], far_recv.at[g], s + 2)

    def far_forward(g):
        return remote(kv.at[g, :, near_rows, :], kv.at[g, :, far_rows, :], fwd_send.at[g], far_recv.at[g], s + 1)

    def back_far_even(g):
        return remote(part.at[g, 0], ret_b.at[g], p0_send.at[g], b_recv.at[g], s - 2)

    def back_far_odd(g):
        return remote(part.at[g, 0], ret_c.at[g], p0_send.at[g], c_recv.at[g], s - 1)

    def back_near(g):
        return remote(part.at[g, 1], ret_a.at[g], p1_send.at[g], a_recv.at[g], s - 1)

    def halo_send(g):
        y_arrive(g, KV_PIECES)

        @pl.when(has_next)
        def _():
            near(g).start()

        @pl.when(even_next)
        def _():
            far_direct(g).start()

    lead = min(Y_LEAD, heads)
    halo_lead = min(HALO_LEAD, heads)
    y_start(0, KV_PIECES)
    for step in range(1, parts):
        stat_copy(step, True).start()
    stat_local = pltpu.make_async_copy(stats_hbm.at[y], stats.at[y], st_loc.at[0])
    stat_local.start()
    for g in range(1, lead):
        y_start(g, KV_PIECES)
        y_start(g - 1, Q_PIECES)
    y_start(lead - 1, Q_PIECES)

    for limit, row in ((2, 0), (1, block)):

        @pl.when(s < limit)
        def _():
            @pl.loop(0, heads)
            def _(g):
                kv[g, :, pl.ds(row, block), :] = jnp.zeros((2, block, HEAD_SIZE), kv.dtype)

    key_tiles = 3 * block // TILE
    reach = LOOKBACK_SPAN // TILE

    def pair_index(t, u):
        return u * (reach + 1) + (t - u)

    for t in range(key_tiles):
        key_doc = jnp.broadcast_to(docs_ref[:, t * TILE:(t + 1) * TILE], (TILE, TILE)).T
        for u in range(2):
            if not 0 <= t - u <= reach:
                continue
            first = 2 * block + u * TILE
            query_doc = docs_ref[:, first:first + TILE]
            gap = (
                (first - t * TILE)
                + lax.broadcasted_iota(jnp.int32, (TILE, TILE), 1)
                - lax.broadcasted_iota(jnp.int32, (TILE, TILE), 0)
            )
            allowed = (key_doc == query_doc) & (gap >= 0) & (gap < LOOKBACK_SPAN)
            bias[pair_index(t, u)] = jnp.where(allowed, 0.0, MASKED)

    for g in range(halo_lead):
        halo_send(g)
    for step in range(1, parts):
        stat_copy(step, False).wait_recv()
    stat_local.wait()

    sources = parts // 2

    def stat_row(g, u, kind):
        found = [
            stats[u * sources + i, g, kind * 2 + j:kind * 2 + j + 1, :]
            for j in range(2)
            for i in range(sources)
        ]
        return jnp.concatenate(found, axis=1) if len(found) > 1 else found[0]

    def tile(g, t, u):
        keys = kv[g, 0, t * TILE:(t + 1) * TILE, :]
        values = kv[g, 1, t * TILE:(t + 1) * TILE, :]
        queries = qd[g, 0, u].reshape(2 * TILE, HEAD_SIZE)
        grads = qd[g, 1, u].reshape(2 * TILE, HEAD_SIZE)
        mask = bias[pair_index(t, u)]
        scores = dot(keys, queries, (1, 1)) * (SCORE_SCALE * LOG2E) - stat_row(g, u, 0)
        prob = jnp.exp2(scores + jnp.concatenate([mask, mask], axis=1))
        prob_grad = dot(values, grads, (1, 1))
        score_grad = (SCORE_SCALE * prob * (prob_grad - stat_row(g, u, 1))).astype(jnp.bfloat16)
        dv = dot(prob.astype(jnp.bfloat16), grads, (1, 0))
        dk = dot(score_grad, queries, (1, 0))
        dq = dot(keys, score_grad, (0, 0))
        if t == u:
            dqt[u] = dq
        else:
            dqt[u] += dq
        first = u == 0 or t == reach + 1
        if t < 2 * block // TILE:
            target, row = acc, t * TILE
        else:
            target, row = own.at[g], t * TILE - 2 * block
        if first:
            target[0, row:row + TILE, :] = dk
            target[1, row:row + TILE, :] = dv
        else:
            target[0, row:row + TILE, :] += dk
            target[1, row:row + TILE, :] += dv

    def combine(g):
        back_far_odd(g).wait_recv()
        part[g, 1] = (part[g, 1].astype(jnp.float32) + ret_c[g].astype(jnp.float32)).astype(jnp.bfloat16)
        back_near(g).start()

    @pl.loop(0, heads)
    def _(g):
        @pl.when(g + lead < heads)
        def _():
            y_start(g + lead, KV_PIECES)
            y_start(g + lead, Q_PIECES)

        @pl.when(g + halo_lead < heads)
        def _():
            halo_send(g + halo_lead)

        @pl.when(has_prev)
        def _():
            near(g).wait_recv()

        @pl.when(even_prev)
        def _():
            far_forward(g).start()

        y_arrive(g, Q_PIECES)

        @pl.when(s >= 2)
        def _():
            far_direct(g).wait_recv()

        own_tile = 2 * block // TILE
        for u in range(2):
            for t in range(u, own_tile):
                tile(g, t, u)
        part[g, 0] = acc[:, 0:block, :].astype(jnp.bfloat16)
        part[g, 1] = acc[:, block:2 * block, :].astype(jnp.bfloat16)

        @pl.when(even_prev)
        def _():
            back_far_even(g).start()

        @pl.when(jnp.logical_not(even))
        def _():
            back_near(g).start()

        @pl.when(jnp.logical_not(even) & (s >= 2))
        def _():
            back_far_odd(g).start()

        for t, u in ((own_tile, 0), (own_tile, 1), (own_tile + 1, 1)):
            tile(g, t, u)
        for u in range(2):
            for j in range(2):
                head_cols = pl.ds(pl.multiple_of((g * 2 + j) * HEAD_SIZE, HEAD_SIZE), HEAD_SIZE)
                dq_ref[u * TILE:(u + 1) * TILE, head_cols] = (
                    dqt[u, :, j * TILE:(j + 1) * TILE].T.astype(jnp.bfloat16)
                )

        @pl.when(even_prev & (g >= 1))
        def _():
            combine(g - 1)

    @pl.when(even_prev)
    def _():
        combine(heads - 1)

    @pl.loop(0, heads)
    def _(g):
        @pl.when(has_next)
        def _():
            back_near(g).wait_recv()
            own[g] += ret_a[g].astype(jnp.float32)

        @pl.when(even_next)
        def _():
            back_far_even(g).wait_recv()
            own[g] += ret_b[g].astype(jnp.float32)

        cols = pl.ds(pl.multiple_of(g * HEAD_SIZE, HEAD_SIZE), HEAD_SIZE)
        dk_ref[:, cols] = own[g, 0].astype(jnp.bfloat16)
        dv_ref[:, cols] = own[g, 1].astype(jnp.bfloat16)

    @pl.loop(0, heads)
    def _(g):
        for copy in y_copies(g, KV_PIECES + Q_PIECES):
            copy.wait_send()

        @pl.when(has_next)
        def _():
            near(g).wait_send()

        @pl.when(even_next)
        def _():
            far_direct(g).wait_send()

        @pl.when(even_prev)
        def _():
            far_forward(g).wait_send()

        @pl.when(s >= 2)
        def _():
            back_far_even(g).wait_send()

        @pl.when(has_prev)
        def _():
            back_near(g).wait_send()

    for step in range(1, parts):
        stat_copy(step, True).wait_send()


def on_device(
    shards, parts,
    rotated_queries, rotated_keys, value_matrix, output_rows, output_gradient, softmax_log_total, doc_ids,
):
    rows = rotated_queries.shape[0]
    query_heads = softmax_log_total.shape[0]
    key_heads = rotated_keys.shape[1] // HEAD_SIZE
    heads = key_heads // parts
    block = rows * parts
    delta = jnp.sum(
        (output_gradient.astype(jnp.float32) * output_rows.astype(jnp.float32)).reshape(rows, query_heads, HEAD_SIZE),
        axis=2,
    ).T
    stats = jnp.concatenate(
        [
            (softmax_log_total * LOG2E).reshape(parts, heads, 2, rows),
            delta.reshape(parts, heads, 2, rows),
        ],
        axis=2,
    )
    padded = jnp.concatenate([jnp.full((LOOKBACK_SPAN,), -1.0, jnp.float32), doc_ids.astype(jnp.float32)])
    docs = lax.dynamic_slice_in_dim(padded, lax.axis_index("seq") * block, 3 * block, 0)[None, :]

    any_spec = pl.BlockSpec(memory_space=pl.ANY)
    vmem = pl.BlockSpec(memory_space=pltpu.VMEM)
    dma = pltpu.SemaphoreType.DMA
    bf16, f32 = jnp.bfloat16, jnp.float32
    back = pltpu.VMEM((heads, 2, block, HEAD_SIZE), bf16)
    pairs = 2 * (LOOKBACK_SPAN // TILE + 1)
    pair_ops = heads * pairs * TILE * 2 * TILE
    return pl.pallas_call(
        functools.partial(kernel, shards, parts, heads),
        out_shape=(
            jax.ShapeDtypeStruct((block, heads * 2 * HEAD_SIZE), bf16),
            jax.ShapeDtypeStruct((block, heads * HEAD_SIZE), bf16),
            jax.ShapeDtypeStruct((block, heads * HEAD_SIZE), bf16),
        ),
        in_specs=[any_spec] * 5 + [vmem],
        out_specs=(vmem, vmem, vmem),
        scratch_shapes=[
            pltpu.VMEM((heads, 2, 3 * block, HEAD_SIZE), bf16),
            pltpu.VMEM((heads, 2, 2, 2, TILE, HEAD_SIZE), bf16),
            pltpu.VMEM((parts, heads, 4, rows), f32),
            pltpu.VMEM((pairs, TILE, TILE), f32),
            pltpu.VMEM((heads, 2, block, HEAD_SIZE), f32),
            pltpu.VMEM((2, 2 * block, HEAD_SIZE), f32),
            pltpu.VMEM((2, HEAD_SIZE, 2 * TILE), f32),
            pltpu.VMEM((heads, 2, 2, block, HEAD_SIZE), bf16),
            back, back, back,
            dma((heads, parts, 6)), dma((heads, parts, 6)), dma((heads, 6)),
            dma((parts,)), dma((parts,)), dma((1,)),
        ] + [dma((heads,))] * 10,
        compiler_params=pltpu.CompilerParams(
            collective_id=0, has_side_effects=True, vmem_limit_bytes=52 * 2 ** 20
        ),
        cost_estimate=pl.CostEstimate(
            flops=pair_ops * HEAD_SIZE * 10, bytes_accessed=16 * 2 ** 20, transcendentals=pair_ops
        ),
    )(rotated_queries, rotated_keys, value_matrix, output_gradient, stats, docs)


def solution(mesh):
    return jax.shard_map(
        functools.partial(on_device, mesh.shape["seq"], mesh.shape["head"]),
        mesh=mesh,
        in_specs=(
            P(("seq", "head"), None),
            P(("seq", "head"), None),
            P(("seq", "head"), None),
            P(("seq", "head"), None),
            P(("seq", "head"), None),
            P(None, ("seq", "head")),
            P(),
        ),
        out_specs=(P("seq", "head"), P("seq", "head"), P("seq", "head")),
        check_vma=False,
    )
```

time: 350 us -> 137 us (0.39); the launches traced: 344 us -> 137 us
  matrix products: 123 us -> 0 us
  Pallas kernels: 0 us -> 121 us
  waiting for transfers between devices: 83.5 us -> 0 us
  local copies, waits for them, and re-layouts: 73.6 us -> 8.62 us
  starting transfers between devices: 49.3 us -> 0 us
  other arithmetic: 12.9 us -> 6.35 us
    dot_general x15 -> x0, matrix products: 123 us -> none  [the longest x3 33.7 us: tile_terms(): jnp.einsum('plmw,mplo->wpo', probability_narrow, grad_four, preferred_ele...]
    pallas_call x0 -> x1, Pallas kernels: none -> 121 us  [on_device(): pl.pallas_call(functools.partial(kernel, shards, parts, heads), out_shape...]
    ppermute x8 -> x0, waiting for transfers between devices: 43.9 us -> none  [shifted(): lax.ppermute(value, axis, [(source, source + steps) for source in range(l...]
    all_to_all x6 -> x0, waiting for transfers between devices: 39.7 us -> none  [the longest x1 20 us: on_device(): lax.all_to_all(rotated_queries, 'head', split_axis=1, concat_axis=0, tile...]
    reshape x11 -> x2, local copies, waits for them, and re-layouts: 37.9 us -> 0.05 us  [the longest x1 0.03 us: on_device(): delta.reshape(parts, heads, 2, rows)]
    ppermute x8 -> x0, starting transfers between devices: 24.9 us -> none  [shifted(): lax.ppermute(value, axis, [(source, source + steps) for source in range(l...]
    all_to_all x6 -> x0, starting transfers between devices: 24.4 us -> none  [the longest x1 4.82 us: on_device(): lax.all_to_all(output_gradient, 'head', split_axis=1, concat_axis=0, tile...]
    unnamed x33 -> x10, local copies, waits for them, and re-layouts: 17.7 us -> 8.41 us
  transfers between devices with their start and end apart: 14 -> 0, of which waited for: 6 -> 0; matrix products, arithmetic and copies ran while one was open for 59% -> 0% of each run, Pallas kernels for 0% -> 0%
where the time goes in v1:
time: 137 us
  Pallas kernels  121 us (88%)
  local copies, waits for them, and re-layouts  8.62 us (6%)
  other arithmetic  6.35 us (5%)
    pallas_call x1, Pallas kernels, on_device(): pl.pallas_call(functools.partial(kernel, shards, parts, heads), out_shape...  121 us
    unnamed x10, local copies, waits for them, and re-layouts  8.41 us
    reduce_sum x1, other arithmetic, on_device(): jnp.sum((output_gradient.astype(jnp.float32) * output_rows.astype(jnp.flo...  3.36 us
    unnamed x1, other arithmetic  2.94 us

profile of v1, /device:TPU:1, one launch (start us, length us, event | category | flops | bytes accessed | tf_op | source)
XLA Modules:
  0.0 136.9 jit_solution(5098882613711846536)
XLA Ops:
  0.6 2.9 %multiply_bitcast_fusion = f32[32,8,32,128]{3,1,2,0:T(8,128)S(1)} fusion(bf16[256,4096]{1,0:T(8,128)(2,1)} %param.10, bf16[256,4096]{1,0:T(8,128)(2,1)} %do_hbm.1), kind=kLoop, calls=%fused_computation | loop fusion | flops 3145728 | bytes 8388608
  3.6 2.7 %copy.11 = f32[32,8,32,128]{3,2,1,0:T(8,128)} copy(f32[32,8,32,128]{3,1,2,0:T(8,128)S(1)} %multiply_bitcast_fusion) | data formatting | bytes 8388608
  6.3 0.0 copy-start.1
  6.3 0.0 copy-start.2
  6.3 3.4 %reduce_sum.9 = f32[256,32]{1,0:T(8,128)S(1)} reduce(f32[256,32,128]{2,1,0:T(8,128)} %bitcast.4, f32[]{:T(128)} %constant.3.clone.1), dimensions={2}, to_apply=%region_0.0 | reduce | flops 1040384 | bytes 4227076 | tf_op jit(solution)/shard_map/reduce_sum | solution.py:382
  9.6 0.1 copy.10
  9.7 0.0 copy-done.1
  9.8 0.0 copy-done.2
  9.9 0.1 pad_dynamic-slice_fusion
  9.9 121.2 %shard_map.94 = (bf16[512,2048]{1,0:T(8,128)(2,1)}, bf16[512,1024]{1,0:T(8,128)(2,1)S(1)}, bf16[512,1024]{1,0:T(8,128)(2,1)}) custom-call(bf16[256,4096]{1,0:T(8,128)(2,1)} %q_hbm.1, bf16[256,2048]{1,0:T(8,128)(2,1)} %k_hbm.1, bf16[256,2048]{1,0:T(8,128)(2,1)} %v_hbm.1, bf16[256,4096]{1,0:T(8,128)(2,1)} %do_hbm.1, ...), custom_call_target="tpu_custom_call" | custom-call | flops 13421772800 | bytes 16777216 | tf_op jit(solution)/shard_map/pallas_call | solution.py:403
  131.1 3.2 %copy.15 = bf16[512,2048]{1,0:T(8,128)(2,1)} copy(bf16[512,2048]{1,0:T(8,128)(2,1)} %get-tuple-element.6) | data formatting | bytes 4194304
  134.3 0.0 copy-start
  134.3 1.0 copy.16
  135.3 0.6 copy-done
  135.9 1.0 copy.17
  (6 shorter events, 0.1 us)
Async XLA Ops:
  6.3 3.5 %copy-start.1 = (f32[32,256]{1,0:T(8,128)S(1)}, f32[32,256]{1,0:T(8,128)}, u32[]{:S(2)}) copy-start(f32[32,256]{1,0:T(8,128)} %param.12) | copy-start | bytes 98308
  6.3 3.6 %copy-start.2 = (s32[8192]{0:T(1024)S(1)}, s32[8192]{0:T(1024)}, u32[]{:S(2)}) copy-start(s32[8192]{0:T(1024)} %param.13) | copy-start | bytes 98308
  134.3 1.6 %copy-start = (bf16[512,1024]{1,0:T(8,128)(2,1)S(1)}, bf16[512,1024]{1,0:T(8,128)(2,1)}, u32[]{:S(2)}) copy-start(bf16[512,1024]{1,0:T(8,128)(2,1)} %get-tuple-element.8) | copy-start | bytes 3145732

commit v2 on v1

--- a/solution.py
+++ b/solution.py
@@ -15,8 +15,9 @@
 LOG2E = math.log2(math.e)
 MASKED = -1e30
 MESH = pl.DeviceIdType.MESH
-Y_LEAD = 4
-HALO_LEAD = 2
+KV_LEAD = 5
+Q_LEAD = 2
+HALO_LEAD = 3
 
 
 def dot(a, b, contract):
@@ -25,9 +26,9 @@
 
 def kernel(
     shards, parts, heads,
-    q_hbm, k_hbm, v_hbm, do_hbm, stats_hbm, docs_ref,
+    q_hbm, k_hbm, v_hbm, do_hbm, o_hbm, lse_ref, docs_ref,
     dq_ref, dk_ref, dv_ref,
-    kv, qd, stats, bias, own, acc, dqt, part, ret_a, ret_b, ret_c,
+    kv, qd, stats, bias, own, acc, dqt, part, ret_a, ret_b, ret_c, o_buf, do_buf, st_src,
     y_send, y_recv, loc, st_send, st_recv, st_loc,
     near_send, near_recv, fardir_send, fwd_send, far_recv,
     p0_send, p1_send, a_recv, b_recv, c_recv,
@@ -133,7 +134,7 @@
         other = lax.rem(y + step, parts)
         source = y if mine else lax.rem(y + parts - step, parts)
         return pltpu.make_async_remote_copy(
-            src_ref=stats_hbm.at[other], dst_ref=stats.at[source],
+            src_ref=st_src.at[other], dst_ref=stats.at[source],
             send_sem=st_send.at[step], recv_sem=st_recv.at[step],
             device_id=at(s, other), device_id_type=MESH,
         )
@@ -173,17 +174,39 @@
         def _():
             far_direct(g).start()
 
-    lead = min(Y_LEAD, heads)
-    halo_lead = min(HALO_LEAD, heads)
+    kv_lead, q_lead, halo_lead = (min(n, heads) for n in (KV_LEAD, Q_LEAD, HALO_LEAD))
     y_start(0, KV_PIECES)
+    o_copy = pltpu.make_async_copy(o_hbm, o_buf, st_loc.at[0])
+    do_copy = pltpu.make_async_copy(do_hbm, do_buf, st_loc.at[1])
+    o_copy.start()
+    do_copy.start()
+    for g in range(1, halo_lead):
+        y_start(g, KV_PIECES)
+
+    def fill_stats(p, target):
+        @pl.loop(0, heads)
+        def _(g):
+            target[g, 0:2, :] = lse_ref[p, g] * LOG2E
+            for j in range(2):
+                cols = pl.ds(pl.multiple_of(((p * heads + g) * 2 + j) * HEAD_SIZE, HEAD_SIZE), HEAD_SIZE)
+                product = o_buf[:, cols].astype(jnp.float32) * do_buf[:, cols].astype(jnp.float32)
+                target[g, 2 + j:3 + j, :] = jnp.sum(product.T, axis=0, keepdims=True)
+
+    o_copy.wait()
+    do_copy.wait()
     for step in range(1, parts):
+        other = lax.rem(y + step, parts)
+        fill_stats(other, st_src.at[other])
         stat_copy(step, True).start()
-    stat_local = pltpu.make_async_copy(stats_hbm.at[y], stats.at[y], st_loc.at[0])
-    stat_local.start()
-    for g in range(1, lead):
-        y_start(g, KV_PIECES)
-        y_start(g - 1, Q_PIECES)
-    y_start(lead - 1, Q_PIECES)
+    for g in range(halo_lead):
+        halo_send(g)
+        if g < q_lead:
+            y_start(g, Q_PIECES)
+        if halo_lead + g < kv_lead:
+            y_start(halo_lead + g, KV_PIECES)
+    for g in range(halo_lead, q_lead):
+        y_start(g, Q_PIECES)
+    fill_stats(y, stats.at[y])
 
     for limit, row in ((2, 0), (1, block)):
 
@@ -214,11 +237,8 @@
             allowed = (key_doc == query_doc) & (gap >= 0) & (gap < LOOKBACK_SPAN)
             bias[pair_index(t, u)] = jnp.where(allowed, 0.0, MASKED)
 
-    for g in range(halo_lead):
-        halo_send(g)
     for step in range(1, parts):
         stat_copy(step, False).wait_recv()
-    stat_local.wait()
 
     sources = parts // 2
 
@@ -266,10 +286,13 @@
 
     @pl.loop(0, heads)
     def _(g):
-        @pl.when(g + lead < heads)
-        def _():
-            y_start(g + lead, KV_PIECES)
-            y_start(g + lead, Q_PIECES)
+        @pl.when(g + kv_lead < heads)
+        def _():
+            y_start(g + kv_lead, KV_PIECES)
+
+        @pl.when(g + q_lead < heads)
+        def _():
+            y_start(g + q_lead, Q_PIECES)
 
         @pl.when(g + halo_lead < heads)
         def _():
@@ -307,6 +330,10 @@
         @pl.when(jnp.logical_not(even) & (s >= 2))
         def _():
             back_far_odd(g).start()
+
+        @pl.when(even_prev & (g >= 1))
+        def _():
+            combine(g - 1)
 
         for t, u in ((own_tile, 0), (own_tile, 1), (own_tile + 1, 1)):
             tile(g, t, u)
@@ -317,10 +344,6 @@
                     dqt[u, :, j * TILE:(j + 1) * TILE].T.astype(jnp.bfloat16)
                 )
 
-        @pl.when(even_prev & (g >= 1))
-        def _():
-            combine(g - 1)
-
     @pl.when(even_prev)
     def _():
         combine(heads - 1)
@@ -375,21 +398,10 @@
     rotated_queries, rotated_keys, value_matrix, output_rows, output_gradient, softmax_log_total, doc_ids,
 ):
     rows = rotated_queries.shape[0]
-    query_heads = softmax_log_total.shape[0]
     key_heads = rotated_keys.shape[1] // HEAD_SIZE
     heads = key_heads // parts
     block = rows * parts
-    delta = jnp.sum(
-        (output_gradient.astype(jnp.float32) * output_rows.astype(jnp.float32)).reshape(rows, query_heads, HEAD_SIZE),
-        axis=2,
-    ).T
-    stats = jnp.concatenate(
-        [
-            (softmax_log_total * LOG2E).reshape(parts, heads, 2, rows),
-            delta.reshape(parts, heads, 2, rows),
-        ],
-        axis=2,
-    )
+    lse = softmax_log_total.reshape(parts, heads, 2, rows)
     padded = jnp.concatenate([jnp.full((LOOKBACK_SPAN,), -1.0, jnp.float32), doc_ids.astype(jnp.float32)])
     docs = lax.dynamic_slice_in_dim(padded, lax.axis_index("seq") * block, 3 * block, 0)[None, :]
 
@@ -407,7 +419,7 @@
             jax.ShapeDtypeStruct((block, heads * HEAD_SIZE), bf16),
             jax.ShapeDtypeStruct((block, heads * HEAD_SIZE), bf16),
         ),
-        in_specs=[any_spec] * 5 + [vmem],
+        in_specs=[any_spec] * 5 + [vmem, vmem],
         out_specs=(vmem, vmem, vmem),
         scratch_shapes=[
             pltpu.VMEM((heads, 2, 3 * block, HEAD_SIZE), bf16),
@@ -419,8 +431,11 @@
             pltpu.VMEM((2, HEAD_SIZE, 2 * TILE), f32),
             pltpu.VMEM((heads, 2, 2, block, HEAD_SIZE), bf16),
             back, back, back,
+            pltpu.VMEM(output_rows.shape, bf16),
+            pltpu.VMEM(output_rows.shape, bf16),
+            pltpu.VMEM((parts, heads, 4, rows), f32),
             dma((heads, parts, 6)), dma((heads, parts, 6)), dma((heads, 6)),
-            dma((parts,)), dma((parts,)), dma((1,)),
+            dma((parts,)), dma((parts,)), dma((2,)),
         ] + [dma((heads,))] * 10,
         compiler_params=pltpu.CompilerParams(
             collective_id=0, has_side_effects=True, vmem_limit_bytes=52 * 2 ** 20
@@ -428,7 +443,7 @@
         cost_estimate=pl.CostEstimate(
             flops=pair_ops * HEAD_SIZE * 10, bytes_accessed=16 * 2 ** 20, transcendentals=pair_ops
         ),
-    )(rotated_queries, rotated_keys, value_matrix, output_gradient, stats, docs)
+    )(rotated_queries, rotated_keys, value_matrix, output_gradient, output_rows, lse, docs)
 
 
 def solution(mesh):

time: 137 us -> 127 us (0.927)
  other arithmetic: 6.35 us -> 0.76 us
  local copies, waits for them, and re-layouts: 8.62 us -> 6.6 us
  Pallas kernels: 121 us -> 119 us
    reduce_sum x1 -> x0, other arithmetic: 3.36 us -> none  [on_device(): jnp.sum((output_gradient.astype(jnp.float32) * output_rows.astype(jnp.flo...]
    unnamed x1 -> x0, other arithmetic: 2.94 us -> none
    unnamed x10 -> x5, local copies, waits for them, and re-layouts: 8.41 us -> 5.73 us
    pallas_call x1, Pallas kernels: 121 us -> 119 us  [on_device(): pl.pallas_call(functools.partial(kernel, shards, parts, heads), out_shape...]
where the time goes in v2:
time: 127 us
  Pallas kernels  119 us (94%)
  local copies, waits for them, and re-layouts  6.6 us (5%)
    pallas_call x1, Pallas kernels, on_device(): pl.pallas_call(functools.partial(kernel, shards, parts, heads), out_shape...  119 us
    unnamed x5, local copies, waits for them, and re-layouts  5.73 us

profile of v2, /device:TPU:1, one launch (start us, length us, event | category | flops | bytes accessed | tf_op | source)
XLA Modules:
  0.0 127.1 jit_solution(8142153691114208267)
XLA Ops:
  0.6 0.8 reshape.9.lse_ref
  1.4 0.8 convert_element_type.3
  2.2 0.1 pad_dynamic-slice_fusion
  2.3 119.0 %shard_map.94 = (bf16[512,2048]{1,0:T(8,128)(2,1)}, bf16[512,1024]{1,0:T(8,128)(2,1)S(1)}, bf16[512,1024]{1,0:T(8,128)(2,1)}) custom-call(bf16[256,4096]{1,0:T(8,128)(2,1)} %q_hbm.1, bf16[256,2048]{1,0:T(8,128)(2,1)} %k_hbm.1, bf16[256,2048]{1,0:T(8,128)(2,1)} %v_hbm.1, bf16[256,4096]{1,0:T(8,128)(2,1)} %do_hbm.1, bf16[256,4096]{1,0:T(8,128)(2,1)} %o_hbm.1, ...), custom_call_target="tpu_custom_call" | custom-call | flops 13421772800 | bytes 16777216 | tf_op jit(solution)/shard_map/pallas_call | solution.py:415
  121.3 3.2 %copy.13 = bf16[512,2048]{1,0:T(8,128)(2,1)} copy(bf16[512,2048]{1,0:T(8,128)(2,1)} %get-tuple-element.6) | data formatting | bytes 4194304
  124.5 0.0 copy-start
  124.5 1.0 copy.14
  125.5 0.6 copy-done
  126.1 1.0 copy.15
  (1 shorter events, 0.0 us)
Async XLA Ops:
  124.5 1.6 %copy-start = (bf16[512,1024]{1,0:T(8,128)(2,1)S(1)}, bf16[512,1024]{1,0:T(8,128)(2,1)}, u32[]{:S(2)}) copy-start(bf16[512,1024]{1,0:T(8,128)(2,1)} %get-tuple-element.8) | copy-start | bytes 3145732

commit v3 on v2

--- a/solution.py
+++ b/solution.py
@@ -15,9 +15,10 @@
 LOG2E = math.log2(math.e)
 MASKED = -1e30
 MESH = pl.DeviceIdType.MESH
-KV_LEAD = 5
+KV_LEAD = 7
 Q_LEAD = 2
-HALO_LEAD = 3
+HALO_LEAD = 5
+KV_FIRST = 3
 
 
 def dot(a, b, contract):
@@ -180,7 +181,8 @@
     do_copy = pltpu.make_async_copy(do_hbm, do_buf, st_loc.at[1])
     o_copy.start()
     do_copy.start()
-    for g in range(1, halo_lead):
+    kv_first = min(KV_FIRST, heads)
+    for g in range(1, kv_first):
         y_start(g, KV_PIECES)
 
     def fill_stats(p, target):
@@ -192,20 +194,25 @@
                 product = o_buf[:, cols].astype(jnp.float32) * do_buf[:, cols].astype(jnp.float32)
                 target[g, 2 + j:3 + j, :] = jnp.sum(product.T, axis=0, keepdims=True)
 
+    halo_send(0)
     o_copy.wait()
     do_copy.wait()
     for step in range(1, parts):
         other = lax.rem(y + step, parts)
         fill_stats(other, st_src.at[other])
         stat_copy(step, True).start()
-    for g in range(halo_lead):
+    started = 0
+    for g in range(1, halo_lead):
+        if kv_first + g - 1 < kv_lead:
+            y_start(kv_first + g - 1, KV_PIECES)
         halo_send(g)
-        if g < q_lead:
-            y_start(g, Q_PIECES)
-        if halo_lead + g < kv_lead:
-            y_start(halo_lead + g, KV_PIECES)
-    for g in range(halo_lead, q_lead):
+        if g % 2 == 1 and started < q_lead:
+            y_start(started, Q_PIECES)
+            started += 1
+    for g in range(started, q_lead):
         y_start(g, Q_PIECES)
+    for g in range(kv_first + halo_lead - 1, kv_lead):
+        y_start(g, KV_PIECES)
     fill_stats(y, stats.at[y])
 
     for limit, row in ((2, 0), (1, block)):
@@ -223,12 +230,12 @@
         return u * (reach + 1) + (t - u)
 
     for t in range(key_tiles):
-        key_doc = jnp.broadcast_to(docs_ref[:, t * TILE:(t + 1) * TILE], (TILE, TILE)).T
+        key_doc = jnp.broadcast_to(docs_ref[:, t * TILE:(t + 1) * TILE].astype(jnp.float32), (TILE, TILE)).T
         for u in range(2):
             if not 0 <= t - u <= reach:
                 continue
             first = 2 * block + u * TILE
-            query_doc = docs_ref[:, first:first + TILE]
+            query_doc = docs_ref[:, first:first + TILE].astype(jnp.float32)
             gap = (
                 (first - t * TILE)
                 + lax.broadcasted_iota(jnp.int32, (TILE, TILE), 1)
@@ -402,7 +409,7 @@
     heads = key_heads // parts
     block = rows * parts
     lse = softmax_log_total.reshape(parts, heads, 2, rows)
-    padded = jnp.concatenate([jnp.full((LOOKBACK_SPAN,), -1.0, jnp.float32), doc_ids.astype(jnp.float32)])
+    padded = jnp.concatenate([jnp.full((LOOKBACK_SPAN,), -1, doc_ids.dtype), doc_ids])
     docs = lax.dynamic_slice_in_dim(padded, lax.axis_index("seq") * block, 3 * block, 0)[None, :]
 
     any_spec = pl.BlockSpec(memory_space=pl.ANY)

time: 127 us -> 127 us (level)
  no operation moved by 1% of the time
where the time goes in v3:
time: 127 us
  Pallas kernels  119 us (94%)
  local copies, waits for them, and re-layouts  7.3 us (6%)
    pallas_call x1, Pallas kernels, on_device(): pl.pallas_call(functools.partial(kernel, shards, parts, heads), out_shape...  119 us
    unnamed x5, local copies, waits for them, and re-layouts  5.73 us

profile of v3, /device:TPU:1, one launch (start us, length us, event | category | flops | bytes accessed | tf_op | source)
XLA Modules:
  0.0 127.0 jit_solution(7265712627766122135)
XLA Ops:
  0.6 0.8 pad_dynamic-slice_fusion
  1.4 0.8 reshape.9.lse_ref
  2.2 119.1 %shard_map.94 = (bf16[512,2048]{1,0:T(8,128)(2,1)}, bf16[512,1024]{1,0:T(8,128)(2,1)S(1)}, bf16[512,1024]{1,0:T(8,128)(2,1)}) custom-call(bf16[256,4096]{1,0:T(8,128)(2,1)} %q_hbm.1, bf16[256,2048]{1,0:T(8,128)(2,1)} %k_hbm.1, bf16[256,2048]{1,0:T(8,128)(2,1)} %v_hbm.1, bf16[256,4096]{1,0:T(8,128)(2,1)} %do_hbm.1, bf16[256,4096]{1,0:T(8,128)(2,1)} %o_hbm.1, ...), custom_call_target="tpu_custom_call" | custom-call | flops 13421772800 | bytes 16777216 | tf_op jit(solution)/shard_map/pallas_call | solution.py:422
  121.3 3.2 %copy.13 = bf16[512,2048]{1,0:T(8,128)(2,1)} copy(bf16[512,2048]{1,0:T(8,128)(2,1)} %get-tuple-element.6) | data formatting | bytes 4194304
  124.5 0.0 copy-start
  124.5 1.0 copy.14
  125.4 0.6 copy-done
  126.1 1.0 copy.15
  (1 shorter events, 0.0 us)
Async XLA Ops:
  124.5 1.6 %copy-start = (bf16[512,1024]{1,0:T(8,128)(2,1)S(1)}, bf16[512,1024]{1,0:T(8,128)(2,1)}, u32[]{:S(2)}) copy-start(bf16[512,1024]{1,0:T(8,128)(2,1)} %get-tuple-element.8) | copy-start | bytes 3145732
